TPU v7x, 32 devices: a whole 2x2x4 slice. The times are simulated.
32 devices in a mesh: seq: 8 (over y, x, core), dp: 4 (over z).
Axes of the slice: x: 2, y: 2, z: 4, core: 2. Of those that a mesh axis runs over, the one named last changes fastest.
Arguments:
- frames: bfloat16 [4, 2048, 1536], P('dp', 'seq'), may hold values from -6 to 6
- lengths: int32 [4], P('dp'), may hold values from 512 to 2048, as said below
- wqkv: bfloat16 [1536, 4608], P(None, 'dp')
- wo: bfloat16 [1536, 1536], replicated, may hold values from -0.15625 to 0.15625
- gain_attn: float32 [1536], replicated, may hold values from 0.1 to 1.9
- gain_conv: float32 [1536], replicated, may hold values from 0.1 to 1.9
- conv_w: float32 [31, 1536], replicated, may hold values from -1 to 1
Outputs:
- block_out: bfloat16 [4, 2048, 1536], P('dp', 'seq')
Inputs may be any that keep to these rules, and one draw needn't show every extreme that they name: `lengths`: at least one utterance has all 2048 frames valid.
All inputs are finite; a program needn't handle non-finite values.
Results may differ from a plain program's by a relative error of at most 0.004.
The roundings to bfloat16 on the way count: a program that leaves them out, or rounds other values in their place, can miss the bound.
Values may be sent and summed in bfloat16 or wider, within the bound.
A program may use at most 64 MiB of HBM per device.

v0:
```python
import jax
import jax.numpy as jnp
from jax import lax
from jax.sharding import PartitionSpec as P

HEADS = 16


def padded_2(array, sides, width):
    for axis, dim in sides:
        count, length = (lax.axis_size(axis), array.shape[dim])
        up = [(i, (i + 1) % count) for i in range(count - 1)]
        down = [(j, i) for i, j in up]
        last = lax.slice_in_dim(array, length - width, length, axis=dim)
        leading = lax.slice_in_dim(array, 0, width, axis=dim)
        before = lax.ppermute(last, axis, up)
        after = lax.ppermute(leading, axis, down)
        array = jnp.concatenate([before, array, after], axis=dim)
    return array


def layer_norm(values, gain):
    values = values.astype(jnp.float32)
    mean = jnp.mean(values, axis=-1, keepdims=True)
    centred = values - mean
    var = jnp.mean(centred * centred, axis=-1, keepdims=True)
    return centred * lax.rsqrt(var + 1e-05) * gain


def attend(query, keys, values, length, head_size):
    scores = jnp.einsum(
        "qhe,khe->hqk", query, keys, preferred_element_type=jnp.float32
    ) * head_size ** (-0.5)
    valid = jnp.arange(keys.shape[0], dtype=jnp.int32) < length
    scores = jnp.where(valid[None, None, :], scores, -1e30)
    top = jnp.max(scores, axis=-1, keepdims=True)
    weights = jnp.exp(scores - top)
    probs = (weights / jnp.sum(weights, axis=-1, keepdims=True)).astype(jnp.bfloat16)
    return jnp.einsum("hqk,khe->qhe", probs, values, preferred_element_type=jnp.float32).astype(
        jnp.bfloat16
    )


def body(frames, lengths, wqkv, wo, gain_attn, gain_conv, conv_w):
    rows = frames[0]
    count = rows.shape[0]
    width = rows.shape[1]
    head_size = width // HEADS
    length = lengths[0]
    normed = layer_norm(rows, gain_attn).astype(jnp.bfloat16)
    qkv = jnp.dot(
        normed, lax.all_gather(wqkv, "dp", axis=1, tiled=True), preferred_element_type=jnp.float32
    ).astype(jnp.bfloat16)
    grouped = qkv.reshape(count, HEADS, 3 * head_size)
    local = lax.all_to_all(grouped, "seq", split_axis=1, concat_axis=0, tiled=True)
    total = local.shape[0]
    local_heads = local.shape[1]
    query = local[:, :, :head_size]
    keys = local[:, :, head_size : 2 * head_size]
    values = local[:, :, 2 * head_size :]
    block = 512
    query_blocks = query.reshape(total // block, block, local_heads, head_size)
    attended = lax.map(
        lambda part_rows: attend(part_rows, keys, values, length, head_size), query_blocks
    )
    attended = attended.reshape(total, local_heads, head_size)
    back = lax.all_to_all(attended, "seq", split_axis=0, concat_axis=1, tiled=True)
    heads_out = back.reshape(count, width)
    mid = rows.astype(jnp.float32) + jnp.dot(heads_out, wo, preferred_element_type=jnp.float32)
    first_frame = lax.axis_index("seq") * count
    positions = first_frame + jnp.arange(count, dtype=jnp.int32)
    valid = (positions < length).astype(jnp.float32)
    conv_in = (layer_norm(mid, gain_conv) * valid[:, None]).astype(jnp.bfloat16)
    reach = (conv_w.shape[0] - 1) // 2
    padded = padded_2(conv_in, (("seq", 0),), reach)
    conv = jnp.zeros((count, width), jnp.float32)
    for tap in range(conv_w.shape[0]):
        conv = conv + conv_w[tap][None, :] * padded[tap : tap + count].astype(jnp.float32)
    result = (mid + conv * jax.nn.sigmoid(conv)).astype(jnp.bfloat16)
    return result[None]


def solution(mesh):
    return jax.shard_map(
        body,
        mesh=mesh,
        in_specs=(P("dp", "seq", None), P("dp"), P(None, "dp"), P(), P(), P(), P()),
        out_specs=P("dp", "seq", None),
        check_vma=False,
    )
```

profile of v0, /device:TPU:0, one launch (start us, length us, event | category | flops | bytes accessed | tf_op | source)
XLA Modules:
  0.0 399.0 jit_solution(8569938863491406058)
XLA Ops:
  6.5 0.0 copy-start
  6.5 0.0 all-gather.2.cloned.1.call-start
  6.5 0.7 all-gather.2.cloned.1.call-update
  7.3 0.4 copy-done
  7.7 0.0 copy-start.4
  7.7 0.2 convert_reduce_fusion
  7.9 0.3 fusion.31
  8.2 247.4 %all-gather.2.cloned.1.call-done = bf16[1536,4608]{1,0:T(8,128)(2,1)} async-done(((bf16[1536,1152]{1,0:T(8,128)(2,1)}), bf16[1536,4608]{1,0:T(8,128)(2,1)}) %all-gather.2.cloned.1.call-update) | async-done | bytes 14155792 | tf_op jit(solution)/shard_map/all_gather | solution.py:52
  255.6 0.0 copy-done.4
  255.6 9.2 %convolution_convert_fusion = bf16[256,4608]{1,0:T(8,128)(2,1)S(1)} fusion(bf16[1536,4608]{1,0:T(8,128)(2,1)} %all-gather.2.cloned.1.call-done, bf16[1,256,1536]{2,1,0:T(8,128)(2,1)S(1)} %copy-done, f32[1536]{0:T(1024)S(1)} %copy-done.4, f32[256]{0:T(256)S(1)} %add_rsqrt_fusion.1, f32[256]{0:T(256)S(1)} %broadcast_multiply_fusion.1), kind=kOutput, calls=%fused_computation.23 | convolution fusion | flops 3627024384 | bytes 17309696 | tf_op jit(solution)/shard_map/dot_general | solution.py:51
  264.8 2.4 copy.23
  267.3 3.7 all-to-all-start
  270.9 29.5 %all-to-all-done = bf16[256,16,288]{0,2,1:T(8,128)(2,1)S(1)} async-done(((bf16[256,16,288]{0,2,1:T(8,128)(2,1)}), bf16[256,16,288]{0,2,1:T(8,128)(2,1)S(1)}, u32[]{:S(2)}, u32[]{:S(2)}) %all-to-all-start) | async-done | bytes 2359328 | tf_op jit(solution)/shard_map/all_to_all | solution.py:55
  300.4 0.3 copy.35
  300.7 0.2 fusion.72
  300.9 0.0 copy-start.1
  300.9 1.0 copy.37
  302.0 0.4 copy-done.1
  302.4 50.0 %while.10 = (s32[]{:T(128)}, bf16[4,512,2,96]{1,3,2,0:T(8,128)(2,1)S(1)}, s32[]{:T(128)}, bf16[4,512,2,96]{1,3,2,0:T(8,128)(2,1)}, bf16[2048,2,96]{0,2,1:T(8,128...) while((s32[]{:T(128)}, bf16[4,512,2,96]{1,3,2,0:T(8,128)(2,1)S(1)}, s32[]{:T(128)}, ...), condition=%wide.region_5.6_spmd, body=%wide.region_2.5_spmd.sunk | while | flops 817991680 | bytes 18756180 | solution.py:63
  302.4 0.7 iota_compare_fusion.2
  303.0 6.9 %fusion.89 = (f32[2,512]{1,0:T(2,128)S(1)}, f32[2,512,2048]{2,1,0:T(8,128)}) fusion(pred[2048]{0:T(1024)(128)(4,1)S(1)} %iota_compare_fusion.2, bf16[2048,2,96]{0,2,1:T(8,128)(2,1)S(1)} %get-tuple-element.173, bf16[4,512,2,96]{1,3,2,0:T(8,128)(2,1)} %get-tuple-element.172, s32[]{:T(128)} %get-tuple-element.162), kind=kOutput, calls=%fused_computation.152.clone.1 | convolution fusion | flops 411043840 | bytes 9378304 | tf_op jit(solution)/shard_map/while/body/eval_jaxpr/sub | solution.py:37
  310.0 4.9 %fusion.90 = bf16[4,512,2,96]{1,3,2,0:T(8,128)(2,1)S(1)} fusion(bf16[4,512,2,96]{1,3,2,0:T(8,128)(2,1)S(1)} %get-tuple-element.163, s32[]{:T(128)} %get-tuple-element.162, bf16[2048,2,96]{0,2,1:T(8,128)(2,1)S(1)} %get-tuple-element.174, f32[2,512,2048]{2,1,0:T(8,128)} %get-tuple-element.153, f32[2,512]{1,0:T(2,128)S(1)} %get-tuple-element.154), kind=kOutput, calls=%fused_computation.11.clone.1 | convolution fusion | flops 406945792 | bytes 9375748 | tf_op jit(solution)/shard_map/while/body/eval_jaxpr/hqk,khe->qhe/dot_general | solution.py:39
  314.9 0.7 iota_compare_fusion.2
  315.5 6.9 %fusion.89 = (f32[2,512]{1,0:T(2,128)S(1)}, f32[2,512,2048]{2,1,0:T(8,128)}) fusion(pred[2048]{0:T(1024)(128)(4,1)S(1)} %iota_compare_fusion.2, bf16[2048,2,96]{0,2,1:T(8,128)(2,1)S(1)} %get-tuple-element.173, bf16[4,512,2,96]{1,3,2,0:T(8,128)(2,1)} %get-tuple-element.172, s32[]{:T(128)} %get-tuple-element.162), kind=kOutput, calls=%fused_computation.152.clone.1 | convolution fusion | flops 411043840 | bytes 9378304 | tf_op jit(solution)/shard_map/while/body/eval_jaxpr/sub | solution.py:37
  322.5 4.9 %fusion.90 = bf16[4,512,2,96]{1,3,2,0:T(8,128)(2,1)S(1)} fusion(bf16[4,512,2,96]{1,3,2,0:T(8,128)(2,1)S(1)} %get-tuple-element.163, s32[]{:T(128)} %get-tuple-element.162, bf16[2048,2,96]{0,2,1:T(8,128)(2,1)S(1)} %get-tuple-element.174, f32[2,512,2048]{2,1,0:T(8,128)} %get-tuple-element.153, f32[2,512]{1,0:T(2,128)S(1)} %get-tuple-element.154), kind=kOutput, calls=%fused_computation.11.clone.1 | convolution fusion | flops 406945792 | bytes 9375748 | tf_op jit(solution)/shard_map/while/body/eval_jaxpr/hqk,khe->qhe/dot_general | solution.py:39
  327.4 0.7 iota_compare_fusion.2
  328.0 6.9 %fusion.89 = (f32[2,512]{1,0:T(2,128)S(1)}, f32[2,512,2048]{2,1,0:T(8,128)}) fusion(pred[2048]{0:T(1024)(128)(4,1)S(1)} %iota_compare_fusion.2, bf16[2048,2,96]{0,2,1:T(8,128)(2,1)S(1)} %get-tuple-element.173, bf16[4,512,2,96]{1,3,2,0:T(8,128)(2,1)} %get-tuple-element.172, s32[]{:T(128)} %get-tuple-element.162), kind=kOutput, calls=%fused_computation.152.clone.1 | convolution fusion | flops 411043840 | bytes 9378304 | tf_op jit(solution)/shard_map/while/body/eval_jaxpr/sub | solution.py:37
  335.0 4.9 %fusion.90 = bf16[4,512,2,96]{1,3,2,0:T(8,128)(2,1)S(1)} fusion(bf16[4,512,2,96]{1,3,2,0:T(8,128)(2,1)S(1)} %get-tuple-element.163, s32[]{:T(128)} %get-tuple-element.162, bf16[2048,2,96]{0,2,1:T(8,128)(2,1)S(1)} %get-tuple-element.174, f32[2,512,2048]{2,1,0:T(8,128)} %get-tuple-element.153, f32[2,512]{1,0:T(2,128)S(1)} %get-tuple-element.154), kind=kOutput, calls=%fused_computation.11.clone.1 | convolution fusion | flops 406945792 | bytes 9375748 | tf_op jit(solution)/shard_map/while/body/eval_jaxpr/hqk,khe->qhe/dot_general | solution.py:39
  339.9 0.7 iota_compare_fusion.2
  340.5 6.9 %fusion.89 = (f32[2,512]{1,0:T(2,128)S(1)}, f32[2,512,2048]{2,1,0:T(8,128)}) fusion(pred[2048]{0:T(1024)(128)(4,1)S(1)} %iota_compare_fusion.2, bf16[2048,2,96]{0,2,1:T(8,128)(2,1)S(1)} %get-tuple-element.173, bf16[4,512,2,96]{1,3,2,0:T(8,128)(2,1)} %get-tuple-element.172, s32[]{:T(128)} %get-tuple-element.162), kind=kOutput, calls=%fused_computation.152.clone.1 | convolution fusion | flops 411043840 | bytes 9378304 | tf_op jit(solution)/shard_map/while/body/eval_jaxpr/sub | solution.py:37
  347.5 4.9 %fusion.90 = bf16[4,512,2,96]{1,3,2,0:T(8,128)(2,1)S(1)} fusion(bf16[4,512,2,96]{1,3,2,0:T(8,128)(2,1)S(1)} %get-tuple-element.163, s32[]{:T(128)} %get-tuple-element.162, bf16[2048,2,96]{0,2,1:T(8,128)(2,1)S(1)} %get-tuple-element.174, f32[2,512,2048]{2,1,0:T(8,128)} %get-tuple-element.153, f32[2,512]{1,0:T(2,128)S(1)} %get-tuple-element.154), kind=kOutput, calls=%fused_computation.11.clone.1 | convolution fusion | flops 406945792 | bytes 9375748 | tf_op jit(solution)/shard_map/while/body/eval_jaxpr/hqk,khe->qhe/dot_general | solution.py:39
  352.4 0.0 copy-start.2
  352.4 2.0 copy.30
  354.4 3.6 all-to-all-start.1
  358.6 0.0 copy-done.2
  358.6 0.3 slice_reduce_fusion.30
  358.9 14.3 %all-to-all-done.1 = bf16[2048,2,96]{2,1,0:T(2,128)(2,1)S(1)} async-done(((bf16[2048,2,96]{2,1,0:T(2,128)(2,1)}), bf16[2048,2,96]{2,1,0:T(2,128)(2,1)S(1)}, u32[]{:S(2)}, u32[]{:S(2)}) %all-to-all-start.1) | async-done | bytes 786464 | tf_op jit(solution)/shard_map/all_to_all | solution.py:67
  373.3 0.7 copy.32
  373.9 3.8 fusion.74
  377.8 0.3 multiply_reduce_fusion
  378.1 0.4 copy-done.3
  378.5 0.4 multiply_convert_fusion
  378.9 1.3 collective-permute-start
  380.2 1.3 collective-permute-start.1
  381.5 0.2 slice_reduce_fusion.29
  381.7 0.0 collective-permute-done
  381.7 2.3 collective-permute-done.1
  384.0 8.2 %fusion.66 = bf16[1,256,1536]{2,1,0:T(8,128)(2,1)} fusion(f32[256,1536]{1,0:T(8,128)S(1)} %get-tuple-element.113, bf16[15,1536]{1,0:T(8,128)(2,1)S(1)} %collective-permute-done.1, bf16[256,1536]{1,0:T(8,128)(2,1)S(1)} %multiply_convert_fusion, f32[1536]{0:T(1024)S(1)} %get-tuple-element.91, f32[1536]{0:T(1024)S(1)} %get-tuple-element.92, ...), kind=kLoop, calls=%fused_computation.115 | loop fusion | flops 73924608 | bytes 3428352 | tf_op jit(solution)/shard_map/broadcast_in_dim | solution.py:80
  (8 shorter events, 0.1 us)
Async XLA Ops:
  6.5 1.1 copy-start
  6.5 249.1 %all-gather.2.cloned.1.call-start = ((), (), s32[]{:S(2)}) async-start(), calls=%async_computation.2 | async-start | bytes 17694720 | tf_op jit(solution)/shard_map/all_gather | solution.py:52
  7.7 247.9 %copy-start.4 = (f32[1536]{0:T(1024)S(1)}, f32[1536]{0:T(1024)}, u32[]{:S(2)}) copy-start(f32[1536]{0:T(1024)} %param.13) | copy-start | bytes 18436
  267.3 33.1 %all-to-all-start = ((bf16[256,16,288]{0,2,1:T(8,128)(2,1)}), bf16[256,16,288]{0,2,1:T(8,128)(2,1)S(1)}, u32[]{:S(2)}, u32[]{:S(2)}) async-start(bf16[256,16,288]{0,2,1:T(8,128)(2,1)} %bitcast.71), calls=%async_computation | async-start | bytes 4718592 | tf_op jit(solution)/shard_map/all_to_all | solution.py:55
  300.9 1.4 copy-start.1
  352.4 6.2 %copy-start.2 = (f32[31,1536]{1,0:T(8,128)S(1)}, f32[31,1536]{1,0:T(8,128)}, u32[]{:S(2)}) copy-start(f32[31,1536]{1,0:T(8,128)} %param.15) | copy-start | bytes 571396
  354.4 18.9 %all-to-all-start.1 = ((bf16[2048,2,96]{2,1,0:T(2,128)(2,1)}), bf16[2048,2,96]{2,1,0:T(2,128)(2,1)S(1)}, u32[]{:S(2)}, u32[]{:S(2)}) async-start(bf16[2048,2,96]{2,1,0:T(2,128)(2,1)} %bitcast.8), calls=%async_computation.1 | async-start | bytes 2097152 | tf_op jit(solution)/shard_map/all_to_all | solution.py:67
  377.8 0.7 copy-start.3
  378.9 2.8 collective-permute-start
  380.2 3.9 collective-permute-start.1
Sparse Core Ops, SparseCore 0:
  8.9 246.6 all-gather.1
where the time goes:
time: 402 us; the launch traced here: 399 us
  waiting for transfers between devices  294 us (73%)
  matrix products  60.3 us (15%)
  between operations  14.2 us (4%)
  other arithmetic  12 us (3%)
  starting transfers between devices  9.8 us (2%)
  local copies, waits for them, and re-layouts  8.37 us (2%)
    all_gather x1, waiting for transfers between devices, body(): lax.all_gather(wqkv, 'dp', axis=1, tiled=True)  247 us
    all_to_all x1, waiting for transfers between devices, body(): lax.all_to_all(grouped, 'seq', split_axis=1, concat_axis=0, tiled=True)  29.5 us
    sub x4, matrix products, attend(): weights = jnp.exp(scores - top)  27.7 us
    dot_general x4, matrix products, attend(): jnp.einsum('hqk,khe->qhe', probs, values, preferred_element_type=jnp.floa...  19.6 us
    all_to_all x1, waiting for transfers between devices, body(): lax.all_to_all(attended, 'seq', split_axis=0, concat_axis=1, tiled=True)  14.3 us
    dot_general x1, matrix products, body(): jnp.dot(normed, lax.all_gather(wqkv, 'dp', axis=1, tiled=True), preferred...  9.23 us
    broadcast_in_dim x1, other arithmetic, body(): return result[None]  8.17 us
  transfers between devices with their start and end apart: 5, of which 4 were waited for; matrix products, arithmetic and copies ran while one was open for 0% of the time, Pallas kernels for 0%

commit v1 on v0

v1 whole, which is shorter than its diff:
```python
import functools

import jax
import jax.numpy as jnp
from jax import lax
from jax.experimental import pallas as pl
from jax.experimental.pallas import tpu as pltpu
from jax.sharding import PartitionSpec as P

HEADS = 16
HALO = 16
MESH = pl.DeviceIdType.MESH
LIMIT = 48 * 1024 * 1024


def reversed_bits(value, count):
    bits = count.bit_length() - 1
    out = 0
    for i in range(bits):
        out = out + (value // (1 << i)) % 2 * (1 << (bits - 1 - i))
    return out


def head_group(seq, dp, n_seq, n_dp):
    column = seq // (n_seq // n_dp)
    return (reversed_bits(dp, n_dp) + column) % n_dp


def exchange_kernel(
    n_seq, n_dp, frames, gain, w_ref, normed_out, w_out, halo_out, own,
    w_sem, halo_send, halo_recv, local_sem, send_sem, recv_sem, forward_send, forward_recv,
):
    me = lax.axis_index("seq")
    dp = lax.axis_index("dp")
    rows = frames.shape[0]
    half = n_seq // 2
    column = me // (n_seq // n_dp)
    source = head_group(me, dp, n_seq, n_dp)
    target = reversed_bits((dp + n_dp - column) % n_dp, n_dp)
    sibling = me + 1 - 2 * (me % 2)
    left = (me + n_seq - 1) % n_seq
    right = (me + 1) % n_seq
    peers = [(me + 2 * i) % n_seq for i in range(1, half)]

    barrier = pltpu.get_barrier_semaphore()
    for other in peers + [sibling, left, right]:
        pl.semaphore_signal(barrier, inc=1, device_id=(other, dp), device_id_type=MESH)

    @pl.when(target != dp)
    def _():
        pl.semaphore_signal(barrier, inc=1, device_id=(me, source), device_id_type=MESH)
        pl.semaphore_signal(barrier, inc=1, device_id=(me, target), device_id_type=MESH)
        pl.semaphore_wait(barrier, len(peers) + 5)

    @pl.when(target == dp)
    def _():
        pl.semaphore_wait(barrier, len(peers) + 3)

    weights = pltpu.make_async_remote_copy(
        src_ref=w_ref, dst_ref=w_out, send_sem=w_sem.at[0], recv_sem=w_sem.at[1],
        device_id=(me, target), device_id_type=MESH,
    )
    kept = pltpu.make_async_copy(w_ref, w_out, w_sem.at[2])

    @pl.when(target != dp)
    def _():
        weights.start()

    @pl.when(target == dp)
    def _():
        kept.start()

    part = 64

    def norm_part(i, carry):
        where = pl.ds(pl.multiple_of(i * part, part), part)
        values = frames[where, :].astype(jnp.float32)
        mean = jnp.mean(values, axis=-1, keepdims=True)
        centred = values - mean
        var = jnp.mean(centred * centred, axis=-1, keepdims=True)
        own[where, :] = (centred * lax.rsqrt(var + 1e-05) * gain[...]).astype(jnp.bfloat16)
        return carry

    lax.fori_loop(0, rows // part, norm_part, 0)

    copies = []
    for i in range(1, half):
        copies.append(pltpu.make_async_remote_copy(
            src_ref=own, dst_ref=normed_out.at[me], send_sem=send_sem.at[i], recv_sem=recv_sem.at[i],
            device_id=(peers[i - 1], dp), device_id_type=MESH,
        ))
    copies.append(pltpu.make_async_remote_copy(
        src_ref=own, dst_ref=normed_out.at[me], send_sem=send_sem.at[0], recv_sem=recv_sem.at[0],
        device_id=(sibling, dp), device_id_type=MESH,
    ))
    copies.append(pltpu.make_async_remote_copy(
        src_ref=frames.at[pl.ds(0, HALO)], dst_ref=halo_out.at[1],
        send_sem=halo_send.at[0], recv_sem=halo_recv.at[0],
        device_id=(left, dp), device_id_type=MESH,
    ))
    copies.append(pltpu.make_async_remote_copy(
        src_ref=frames.at[pl.ds(rows - HALO, HALO)], dst_ref=halo_out.at[0],
        send_sem=halo_send.at[1], recv_sem=halo_recv.at[1],
        device_id=(right, dp), device_id_type=MESH,
    ))
    for copy in copies:
        copy.start()
    local = pltpu.make_async_copy(own, normed_out.at[me], local_sem)
    local.start()

    forwards = []
    for i in range(1, half):
        origin = (me + n_seq - 2 * i) % n_seq
        copies[i - 1].wait_recv()
        forward = pltpu.make_async_remote_copy(
            src_ref=normed_out.at[origin], dst_ref=normed_out.at[origin],
            send_sem=forward_send.at[i], recv_sem=forward_recv.at[i],
            device_id=(sibling, dp), device_id_type=MESH,
        )
        forward.start()
        forwards.append(forward)
    for copy in copies[half - 1:]:
        copy.wait_recv()
    for forward in forwards:
        forward.wait_recv()
    for copy in copies:
        copy.wait_send()
    for forward in forwards:
        forward.wait_send()
    local.wait()

    @pl.when(target != dp)
    def _():
        weights.wait()

    @pl.when(target == dp)
    def _():
        kept.wait()


def exchange(frames, gain, w, n_seq, n_dp):
    rows, width = frames.shape
    return pl.pallas_call(
        functools.partial(exchange_kernel, n_seq, n_dp),
        out_shape=(
            jax.ShapeDtypeStruct((n_seq, rows, width), jnp.bfloat16),
            jax.ShapeDtypeStruct(w.shape, jnp.bfloat16),
            jax.ShapeDtypeStruct((2, HALO, width), jnp.bfloat16),
        ),
        in_specs=[
            pl.BlockSpec(memory_space=pltpu.VMEM),
            pl.BlockSpec(memory_space=pltpu.VMEM),
            pl.BlockSpec(memory_space=pl.ANY),
        ],
        out_specs=(pl.BlockSpec(memory_space=pl.ANY),) * 3,
        scratch_shapes=[
            pltpu.VMEM((rows, width), jnp.bfloat16),
            pltpu.SemaphoreType.DMA((3,)),
            pltpu.SemaphoreType.DMA((2,)),
            pltpu.SemaphoreType.DMA((2,)),
            pltpu.SemaphoreType.DMA,
            pltpu.SemaphoreType.DMA((n_seq // 2,)),
            pltpu.SemaphoreType.DMA((n_seq // 2,)),
            pltpu.SemaphoreType.DMA((n_seq // 2,)),
            pltpu.SemaphoreType.DMA((n_seq // 2,)),
        ],
        compiler_params=pltpu.CompilerParams(collective_id=0, has_side_effects=True, vmem_limit_bytes=LIMIT),
    )(frames, gain, w)


def attend_kernel(head_size, n_heads, block, length_ref, qkv, out, keys_t, values, queries):
    step = pl.program_id(0)
    total = qkv.shape[0]
    wide = 128
    scale = head_size ** (-0.5) * 1.4426950408889634

    @pl.when(step == 0)
    def _():
        out[0:HALO, :] = jnp.zeros((HALO, out.shape[1]), out.dtype)
        out[total + HALO : total + 2 * HALO, :] = jnp.zeros((HALO, out.shape[1]), out.dtype)
        length = length_ref[0]
        part = 256

        def prepare(i, carry):
            start = pl.multiple_of(i * part, part)
            where = pl.ds(start, part)
            extra = lax.broadcasted_iota(jnp.int32, (part, wide - head_size), 1)
            row = start + lax.broadcasted_iota(jnp.int32, (part, wide - head_size), 0)
            first = extra == 0
            ones = jnp.where(first, 1.0, 0.0).astype(jnp.bfloat16)
            bias = jnp.where(first & (row >= length), -1e30, 0.0).astype(jnp.bfloat16)
            for h in range(n_heads):
                base = h * 3 * head_size
                q = qkv[where, base : base + head_size]
                k = qkv[where, base + head_size : base + 2 * head_size]
                v = qkv[where, base + 2 * head_size : base + 3 * head_size]
                queries[h, where, :] = jnp.concatenate([q, ones], axis=1)
                values[h, where, :] = jnp.concatenate([v, ones], axis=1)
                keys_t[h, :, where] = jnp.concatenate([k, bias], axis=1).T
            return carry

        lax.fori_loop(0, total // part, prepare, 0)

    start = pl.multiple_of(step * block, block)
    where = pl.ds(start, block)
    outs = []
    for h in range(n_heads):
        scores = jnp.dot(queries[h, where, :], keys_t[h], preferred_element_type=jnp.float32)
        top = jnp.max(scores, axis=-1, keepdims=True)
        weights = jnp.exp2((scores - top) * scale).astype(jnp.bfloat16)
        summed = jnp.dot(weights, values[h], preferred_element_type=jnp.float32)
        outs.append((summed[:, :head_size] / summed[:, head_size : head_size + 1]).astype(jnp.bfloat16))
    out[pl.ds(pl.multiple_of(start + HALO, HALO), block), :] = jnp.concatenate(outs, axis=1)


def attend(qkv, length, head_size):
    total, columns = qkv.shape
    n_heads = columns // (3 * head_size)
    block = 256
    return pl.pallas_call(
        functools.partial(attend_kernel, head_size, n_heads, block),
        grid=(total // block,),
        out_shape=jax.ShapeDtypeStruct((total + 2 * HALO, n_heads * head_size), jnp.bfloat16),
        in_specs=[
            pl.BlockSpec(memory_space=pltpu.SMEM),
            pl.BlockSpec((total, columns), lambda i: (0, 0)),
        ],
        out_specs=pl.BlockSpec((total + 2 * HALO, n_heads * head_size), lambda i: (0, 0)),
        scratch_shapes=[
            pltpu.VMEM((n_heads, 128, total), jnp.bfloat16),
            pltpu.VMEM((n_heads, total, 128), jnp.bfloat16),
            pltpu.VMEM((n_heads, total, 128), jnp.bfloat16),
        ],
        compiler_params=pltpu.CompilerParams(vmem_limit_bytes=LIMIT),
    )(length, qkv)


def return_kernel(n_seq, count, attended, parts, local_sem, send_sem, recv_sem):
    me = lax.axis_index("seq")
    dp = lax.axis_index("dp")
    others = [(me + i) % n_seq for i in range(1, n_seq)]
    barrier = pltpu.get_barrier_semaphore()
    for other in others:
        pl.semaphore_signal(barrier, inc=1, device_id=(other, dp), device_id_type=MESH)
    pl.semaphore_wait(barrier, n_seq - 1)

    def rows_of(owner):
        return attended.at[pl.ds(pl.multiple_of(owner * count, count), count + 2 * HALO)]

    copies = []
    for i, other in enumerate(others):
        copy = pltpu.make_async_remote_copy(
            src_ref=rows_of(other), dst_ref=parts.at[me], send_sem=send_sem.at[i], recv_sem=recv_sem.at[i],
            device_id=(other, dp), device_id_type=MESH,
        )
        copy.start()
        copies.append(copy)
    local = pltpu.make_async_copy(rows_of(me), parts.at[me], local_sem)
    local.start()
    for copy in copies:
        copy.wait()
    local.wait()


def send_back(attended, n_seq, count):
    return pl.pallas_call(
        functools.partial(return_kernel, n_seq, count),
        out_shape=jax.ShapeDtypeStruct((n_seq, count + 2 * HALO, attended.shape[1]), jnp.bfloat16),
        in_specs=[pl.BlockSpec(memory_space=pl.ANY)],
        out_specs=pl.BlockSpec(memory_space=pl.ANY),
        scratch_shapes=[
            pltpu.SemaphoreType.DMA,
            pltpu.SemaphoreType.DMA((n_seq - 1,)),
            pltpu.SemaphoreType.DMA((n_seq - 1,)),
        ],
        compiler_params=pltpu.CompilerParams(collective_id=1, has_side_effects=True, vmem_limit_bytes=LIMIT),
    )(attended)


def finish_kernel(n_seq, n_dp, length_ref, parts, frames, halo, wo, gain, conv_w, out, mid, padded):
    me = lax.axis_index("seq")
    dp = lax.axis_index("dp")
    count, width = frames.shape
    tall = count + 2 * HALO
    share = n_seq // n_dp
    depth = parts.shape[2]
    taps = conv_w.shape[0]
    reach = (taps - 1) // 2
    cut = 512

    for c in range(width // cut):
        columns = slice(c * cut, (c + 1) * cut)
        total = jnp.concatenate(
            [halo[0, :, columns], frames[:, columns], halo[1, :, columns]], axis=0
        ).astype(jnp.float32)
        for s in range(n_seq):
            slot = head_group(s, dp, n_seq, n_dp) * share + s % share
            rows = pl.ds(pl.multiple_of(slot * depth, depth), depth)
            total = total + jnp.dot(parts[s], wo[rows, columns], preferred_element_type=jnp.float32)
        mid[:, columns] = total

    part = 32

    def norm_part(i, carry):
        start = pl.multiple_of(i * part, part)
        where = pl.ds(start, part)
        values = mid[where, :]
        mean = jnp.mean(values, axis=-1, keepdims=True)
        centred = values - mean
        var = jnp.mean(centred * centred, axis=-1, keepdims=True)
        position = me * count - HALO + start + lax.broadcasted_iota(jnp.int32, (part, 1), 0)
        valid = (position >= 0) & (position < length_ref[0])
        normed = centred * lax.rsqrt(var + 1e-05) * gain[...]
        padded[where, :] = jnp.where(valid, normed, 0.0).astype(jnp.bfloat16).astype(jnp.float32)
        return carry

    lax.fori_loop(0, tall // part, norm_part, 0)

    lanes = 128

    def conv_part(c, carry):
        columns = pl.ds(pl.multiple_of(c * lanes, lanes), lanes)
        for half in range(count // 128):
            base = half * 128
            conv = jnp.zeros((128, lanes), jnp.float32)
            for tap in range(taps):
                first = base + HALO - reach + tap
                conv = conv + conv_w[tap : tap + 1, columns] * padded[first : first + 128, columns]
            result = mid[base + HALO : base + HALO + 128, columns] + conv * jax.nn.sigmoid(conv)
            out[base : base + 128, columns] = result.astype(jnp.bfloat16)
        return carry

    lax.fori_loop(0, width // lanes, conv_part, 0)


def finish(length, parts, frames, halo, wo, gain, conv_w, n_seq, n_dp):
    count, width = frames.shape
    return pl.pallas_call(
        functools.partial(finish_kernel, n_seq, n_dp),
        out_shape=jax.ShapeDtypeStruct((count, width), jnp.bfloat16),
        in_specs=[pl.BlockSpec(memory_space=pltpu.SMEM)] + [pl.BlockSpec(memory_space=pltpu.VMEM)] * 6,
        out_specs=pl.BlockSpec(memory_space=pltpu.VMEM),
        scratch_shapes=[
            pltpu.VMEM((count + 2 * HALO, width), jnp.float32),
            pltpu.VMEM((count + 2 * HALO, width), jnp.float32),
        ],
        compiler_params=pltpu.CompilerParams(vmem_limit_bytes=LIMIT),
    )(length, parts, frames, halo, wo, gain, conv_w)


def body(n_seq, n_dp, frames, lengths, wqkv, wo, gain_attn, gain_conv, conv_w):
    rows = frames[0]
    count, width = rows.shape
    head_size = width // HEADS
    share = n_seq // n_dp
    columns = wqkv.shape[1] // share
    seq = lax.axis_index("seq")
    w = lax.dynamic_slice_in_dim(wqkv, seq % share * columns, columns, axis=1)
    normed, w, halo = exchange(rows, gain_attn[None], w, n_seq, n_dp)
    qkv = jnp.dot(
        normed.reshape(n_seq * count, width), w, preferred_element_type=jnp.float32
    ).astype(jnp.bfloat16)
    attended = attend(qkv, lengths, head_size)
    parts = send_back(attended, n_seq, count)
    return finish(lengths, parts, rows, halo, wo, gain_conv[None], conv_w, n_seq, n_dp)[None]


def solution(mesh):
    return jax.shard_map(
        functools.partial(body, mesh.shape["seq"], mesh.shape["dp"]),
        mesh=mesh,
        in_specs=(P("dp", "seq", None), P("dp"), P(None, "dp"), P(), P(), P(), P()),
        out_specs=P("dp", "seq", None),
        check_vma=False,
    )
```

time: 402 us -> 116 us (0.29)
  waiting for transfers between devices: 294 us -> 0 us
  Pallas kernels: 0 us -> 96.8 us
  matrix products: 60.3 us -> 8.12 us
  between operations: 14.2 us -> 0.76 us
  other arithmetic: 12 us -> 0 us
  starting transfers between devices: 9.8 us -> 0 us
    all_gather x1 -> x0, waiting for transfers between devices: 247 us -> none  [body(): lax.all_gather(wqkv, 'dp', axis=1, tiled=True)]
    pallas_call x0 -> x4, Pallas kernels: none -> 96.8 us  [the longest x1 44.8 us: exchange(): pl.pallas_call(functools.partial(exchange_kernel, n_seq, n_dp), out_shape...]
    all_to_all x2 -> x0, waiting for transfers between devices: 43.8 us -> none  [the longest x1 29.5 us: body(): lax.all_to_all(grouped, 'seq', split_axis=1, concat_axis=0, tiled=True)]
    sub x4 -> x0, matrix products: 27.7 us -> none  [attend(): weights = jnp.exp(scores - top)]
    dot_general x6 -> x1, matrix products: 32.6 us -> 8.12 us  [body(): jnp.dot(normed.reshape(n_seq * count, width), w, preferred_element_type=j...]
    broadcast_in_dim x2 -> x0, other arithmetic: 8.17 us -> none  [the longest x1 8.17 us: body(): return result[None]]
    all_to_all x2 -> x0, starting transfers between devices: 7.21 us -> none  [the longest x1 3.65 us: body(): lax.all_to_all(grouped, 'seq', split_axis=1, concat_axis=0, tiled=True)]
  transfers between devices with their start and end apart: 5 -> 0, of which waited for: 4 -> 0; matrix products, arithmetic and copies ran while one was open for 0% -> 0% of each run, Pallas kernels for 0% -> 0%
where the time goes in v1:
time: 116 us
  Pallas kernels  96.8 us (83%)
  local copies, waits for them, and re-layouts  9.84 us (8%)
  matrix products  8.12 us (7%)
    pallas_call x1, Pallas kernels, exchange(): pl.pallas_call(functools.partial(exchange_kernel, n_seq, n_dp), out_shape...  44.8 us
    pallas_call x1, Pallas kernels, send_back(): pl.pallas_call(functools.partial(return_kernel, n_seq, count), out_shape=...  19.9 us
    pallas_call x1, Pallas kernels, attend(): pl.pallas_call(functools.partial(attend_kernel, head_size, n_heads, block...  16.6 us
    pallas_call x1, Pallas kernels, finish(): pl.pallas_call(functools.partial(finish_kernel, n_seq, n_dp), out_shape=j...  15.5 us
    dot_general x1, matrix products, body(): jnp.dot(normed.reshape(n_seq * count, width), w, preferred_element_type=j...  8.12 us
    unnamed x18, local copies, waits for them, and re-layouts  4.59 us
    convert_element_type x1, local copies, waits for them, and re-layouts, body(): qkv = jnp.dot(normed.reshape(n_seq * count, width), w, preferred_element_...  4.33 us

profile of v1, /device:TPU:0, one launch (start us, length us, event | category | flops | bytes accessed | tf_op | source)
XLA Modules:
  0.0 115.6 jit_solution(1043446824229484512)
XLA Ops:
  0.0 0.0 copy-start
  0.0 0.0 copy-start.7
  0.0 2.0 %copy-done = bf16[1536,1152]{1,0:T(8,128)(2,1)S(1)} copy-done((bf16[1536,1152]{1,0:T(8,128)(2,1)S(1)}, bf16[1536,1152]{1,0:T(8,128)(2,1)}, u32[]{:S(2)}) %copy-start) | copy-done | bytes 3538968
  2.0 0.0 copy-start.2
  2.0 0.9 constant_dynamic-slice_fusion.w_ref
  2.9 0.0 copy-done.7
  2.9 0.2 copy-done.2
  3.1 44.8 %shard_map.73 = (bf16[8,256,1536]{2,1,0:T(8,128)(2,1)}, bf16[1536,576]{1,0:T(8,128)(2,1)S(1)}, bf16[2,16,1536]{2,1,0:T(8,128)(2,1)S(1)}) custom-call(bf16[256,1536]{1,0:T(8,128)(2,1)S(1)} %bitcast.5, f32[1,1536]{1,0:T(1,128)S(1)} %broadcast_in_dim.9.gain, bf16[1536,576]{1,0:T(8,128)(2,1)S(1)} %constant_dynamic-slice_fusion.w_ref), custom_call_target="tpu_custom_call" | custom-call | tf_op jit(solution)/shard_map/pallas_call | solution.py:143
  47.9 0.0 copy-start.5
  47.9 0.6 copy-done.5
  48.5 8.1 %convolution_convert_fusion = bf16[2048,576]{0,1:T(8,128)(2,1)} fusion(bf16[2048,1536]{1,0:T(8,128)(2,1)} %bitcast.7, bf16[1536,576]{1,0:T(8,128)(2,1)S(1)} %get-tuple-element.9), kind=kOutput, calls=%fused_computation | convolution fusion | flops 3625058304 | bytes 10420224 | tf_op jit(solution)/shard_map/dot_general | solution.py:360
  56.7 4.3 %copy.9.qkv = bf16[2048,576]{1,0:T(8,128)(2,1)} copy(bf16[2048,576]{0,1:T(8,128)(2,1)} %convolution_convert_fusion) | data formatting | bytes 4718592 | tf_op jit(solution)/shard_map/convert_element_type | solution.py:362
  61.6 0.0 copy-start.1
  61.7 1.7 %copy-done.1 = bf16[2048,576]{1,0:T(8,128)(2,1)S(1)} copy-done((bf16[2048,576]{1,0:T(8,128)(2,1)S(1)}, bf16[2048,576]{1,0:T(8,128)(2,1)}, u32[]{:S(2)}) %copy-start.1) | copy-done | bytes 2359320
  63.4 0.0 copy-start.8
  63.4 0.0 copy-start.3
  63.4 0.0 copy-start.4
  63.4 0.0 copy-start.6
  63.4 16.6 %shard_map.74.attended = bf16[2080,192]{1,0:T(8,128)(2,1)S(1)} custom-call(s32[1]{0:T(128)S(6)} %copy.10.length_ref, bf16[2048,576]{1,0:T(8,128)(2,1)S(1)} %copy-done.1), custom_call_target="tpu_custom_call" | custom-call | tf_op jit(solution)/shard_map/pallas_call | solution.py:220
  80.0 19.9 %shard_map.75.parts = bf16[8,288,192]{2,1,0:T(8,128)(2,1)S(1)} custom-call(bf16[2080,192]{1,0:T(8,128)(2,1)S(1)} %shard_map.74.attended), custom_call_target="tpu_custom_call" | custom-call | tf_op jit(solution)/shard_map/pallas_call | solution.py:266
  100.0 0.0 copy-done.8
  100.0 0.0 copy-done.3
  100.0 0.0 copy-done.4
  100.0 0.0 copy-done.6
  100.0 15.5 %shard_map.76 = bf16[256,1536]{1,0:T(8,128)(2,1)} custom-call(s32[1]{0:T(128)S(6)} %copy.10.length_ref, bf16[8,288,192]{2,1,0:T(8,128)(2,1)S(1)} %shard_map.75.parts, bf16[256,1536]{1,0:T(8,128)(2,1)S(1)} %bitcast.6, bf16[2,16,1536]{2,1,0:T(8,128)(2,1)S(1)} %copy-done.6, bf16[1536,1536]{1,0:T(8,128)(2,1)} %wo.1, f32[1,1536]{1,0:T(1,128)S(1)} %broadcast_in_dim.10.gain, ...), custom_call_target="tpu_custom_call" | custom-call | tf_op jit(solution)/shard_map/pallas_call | solution.py:338
  (2 shorter events, 0.0 us)
Async XLA Ops:
  0.0 2.0 %copy-start = (bf16[1536,1152]{1,0:T(8,128)(2,1)S(1)}, bf16[1536,1152]{1,0:T(8,128)(2,1)}, u32[]{:S(2)}) copy-start(bf16[1536,1152]{1,0:T(8,128)(2,1)} %param.9) | copy-start | bytes 10616836
  0.0 2.9 %copy-start.7 = (f32[1536]{0:T(1024)S(1)}, f32[1536]{0:T(1024)}, u32[]{:S(2)}) copy-start(f32[1536]{0:T(1024)} %param.11) | copy-start | bytes 18436
  2.0 1.1 copy-start.2
  47.9 0.6 copy-start.5
  61.6 1.7 %copy-start.1 = (bf16[2048,576]{1,0:T(8,128)(2,1)S(1)}, bf16[2048,576]{1,0:T(8,128)(2,1)}, u32[]{:S(2)}) copy-start(bf16[2048,576]{1,0:T(8,128)(2,1)} %copy.9.qkv) | copy-start | bytes 7077892
  63.4 36.6 %copy-start.8 = (f32[1536]{0:T(1024)S(1)}, f32[1536]{0:T(1024)}, u32[]{:S(2)}) copy-start(f32[1536]{0:T(1024)} %param.12) | copy-start | bytes 18436
  63.4 36.6 %copy-start.3 = (bf16[1,256,1536]{2,1,0:T(8,128)(2,1)S(1)}, bf16[1,256,1536]{2,1,0:T(8,128)(2,1)}, u32[]{:S(2)}) copy-start(bf16[1,256,1536]{2,1,0:T(8,128)(2,1)} %param.7) | copy-start | bytes 2359300
  63.4 36.6 %copy-start.4 = (f32[31,1536]{1,0:T(8,128)S(1)}, f32[31,1536]{1,0:T(8,128)}, u32[]{:S(2)}) copy-start(f32[31,1536]{1,0:T(8,128)} %conv_w.1) | copy-start | bytes 571396
  63.4 36.6 %copy-start.6 = (bf16[2,16,1536]{2,1,0:T(8,128)(2,1)S(1)}, bf16[2,16,1536]{2,1,0:T(8,128)(2,1)}, u32[]{:S(2)}) copy-start(bf16[2,16,1536]{2,1,0:T(8,128)(2,1)} %copy-done.5) | copy-start | bytes 294916

commit v2 on v1

v2 whole, which is shorter than its diff:
```python
import functools

import jax
import jax.numpy as jnp
from jax import lax
from jax.experimental import pallas as pl
from jax.experimental.pallas import tpu as pltpu
from jax.sharding import PartitionSpec as P

HEADS = 16
HALO = 16
MESH = pl.DeviceIdType.MESH
LIMIT = 48 * 1024 * 1024


def reversed_bits(value, count):
    bits = count.bit_length() - 1
    out = 0
    for i in range(bits):
        out = out + (value // (1 << i)) % 2 * (1 << (bits - 1 - i))
    return out


def head_group(seq, dp, n_seq, n_dp):
    column = seq // (n_seq // n_dp)
    return (reversed_bits(dp, n_dp) + column) % n_dp


def attention_kernel(
    n_seq, n_dp, head_size, length_ref, frames_ref, gain, w_ref, parts, halo_out,
    frames, normed, w, acc, keys_t, values, queries, attended,
    frame_sem, w_send, w_recv, halo_send, halo_recv,
    send_sem, recv_sem, forward_send, forward_recv, back_send, back_recv,
):
    me = lax.axis_index("seq")
    dp = lax.axis_index("dp")
    rows, width = frames.shape
    total = n_seq * rows
    half = n_seq // 2
    column = me // (n_seq // n_dp)
    source = head_group(me, dp, n_seq, n_dp)
    target = reversed_bits((dp + n_dp - column) % n_dp, n_dp)
    sibling = me + 1 - 2 * (me % 2)
    left = (me + n_seq - 1) % n_seq
    right = (me + 1) % n_seq
    peers = [(me + 2 * i) % n_seq for i in range(1, half)]
    n_heads = w.shape[1] // (3 * head_size)
    wide = 128

    load = pltpu.make_async_copy(frames_ref, frames, frame_sem)
    load.start()
    barrier = pltpu.get_barrier_semaphore()
    for i in range(1, n_seq):
        pl.semaphore_signal(barrier, inc=1, device_id=((me + i) % n_seq, dp), device_id_type=MESH)

    @pl.when(target != dp)
    def _():
        pl.semaphore_signal(barrier, inc=1, device_id=(me, source), device_id_type=MESH)
        pl.semaphore_signal(barrier, inc=1, device_id=(me, target), device_id_type=MESH)
        pl.semaphore_wait(barrier, n_seq + 1)

    @pl.when(target == dp)
    def _():
        pl.semaphore_wait(barrier, n_seq - 1)

    pieces = 3
    deep = width // pieces

    def weights(c):
        where = pl.ds(c * deep, deep)
        return pltpu.make_async_remote_copy(
            src_ref=w_ref.at[where], dst_ref=w.at[where], send_sem=w_send.at[c], recv_sem=w_recv.at[c],
            device_id=(me, target), device_id_type=MESH,
        )

    def kept(c):
        where = pl.ds(c * deep, deep)
        return pltpu.make_async_copy(w_ref.at[where], w.at[where], w_recv.at[c])

    @pl.when(target != dp)
    def _():
        for c in range(pieces):
            weights(c).start()

    @pl.when(target == dp)
    def _():
        for c in range(pieces):
            kept(c).start()

    load.wait()
    part = 64

    def norm_part(i, carry):
        where = pl.ds(pl.multiple_of(i * part, part), part)
        numbers = frames[where, :].astype(jnp.float32)
        mean = jnp.mean(numbers, axis=-1, keepdims=True)
        centred = numbers - mean
        var = jnp.mean(centred * centred, axis=-1, keepdims=True)
        normed[me, where, :] = (centred * lax.rsqrt(var + 1e-05) * gain[...]).astype(jnp.bfloat16)
        return carry

    lax.fori_loop(0, rows // part, norm_part, 0)

    copies = []
    for i in range(half):
        copies.append(pltpu.make_async_remote_copy(
            src_ref=normed.at[me], dst_ref=normed.at[me], send_sem=send_sem.at[i], recv_sem=recv_sem.at[i],
            device_id=(peers[i - 1] if i else sibling, dp), device_id_type=MESH,
        ))
    copies.append(pltpu.make_async_remote_copy(
        src_ref=frames.at[pl.ds(0, HALO)], dst_ref=halo_out.at[1],
        send_sem=halo_send.at[0], recv_sem=halo_recv.at[0],
        device_id=(left, dp), device_id_type=MESH,
    ))
    copies.append(pltpu.make_async_remote_copy(
        src_ref=frames.at[pl.ds(rows - HALO, HALO)], dst_ref=halo_out.at[0],
        send_sem=halo_send.at[1], recv_sem=halo_recv.at[1],
        device_id=(right, dp), device_id_type=MESH,
    ))
    for copy in copies[1:] + copies[:1]:
        copy.start()

    forwards = []
    for i in range(1, half):
        origin = (me + n_seq - 2 * i) % n_seq
        copies[i].wait_recv()
        forward = pltpu.make_async_remote_copy(
            src_ref=normed.at[origin], dst_ref=normed.at[origin],
            send_sem=forward_send.at[i], recv_sem=forward_recv.at[i],
            device_id=(sibling, dp), device_id_type=MESH,
        )
        forward.start()
        forwards.append(forward)
    for copy in copies[:1] + copies[half:]:
        copy.wait_recv()
    for forward in forwards:
        forward.wait_recv()

    for c in range(pieces):
        @pl.when(target != dp)
        def _():
            weights(c).wait()

        @pl.when(target == dp)
        def _():
            kept(c).wait()

        depth = slice(c * deep, (c + 1) * deep)

        def product(s, carry):
            where = pl.ds(pl.multiple_of(s * rows, rows), rows)
            term = jnp.dot(normed[s, :, depth], w[depth, :], preferred_element_type=jnp.float32)
            if c:
                term = acc[where, :] + term
            if c < pieces - 1:
                acc[where, :] = term
                return carry
            qkv = term.astype(jnp.bfloat16)
            extra = lax.broadcasted_iota(jnp.int32, (rows, wide - head_size), 1)
            row = s * rows + lax.broadcasted_iota(jnp.int32, (rows, wide - head_size), 0)
            first = extra == 0
            ones = jnp.where(first, 1.0, 0.0).astype(jnp.bfloat16)
            bias = jnp.where(first & (row >= length_ref[0]), -1e30, 0.0).astype(jnp.bfloat16)
            for h in range(n_heads):
                q, k, v = (
                    qkv[:, (3 * h + p) * head_size : (3 * h + p + 1) * head_size] for p in range(3)
                )
                queries[h, where, :] = jnp.concatenate([q, ones], axis=1)
                values[h, where, :] = jnp.concatenate([v, ones], axis=1)
                keys_t[h, :, where] = jnp.concatenate([k, bias], axis=1).T
            return carry

        lax.fori_loop(0, n_seq, product, 0)

    scale = head_size ** (-0.5) * 1.4426950408889634
    places = [(0, rows, HALO), (rows - HALO, HALO, 0), (0, HALO, rows + HALO)]

    def back(kind, offset):
        dest = (me + offset) % n_seq
        block = (dest + n_seq - (0, 1, n_seq - 1)[kind]) % n_seq
        first, size, at = places[kind]
        src = attended.at[pl.ds(pl.multiple_of(block * rows + first, HALO), size)]
        dst = parts.at[me, pl.ds(at, size)]
        remote = pltpu.make_async_remote_copy(
            src_ref=src, dst_ref=dst, send_sem=back_send.at[kind, offset], recv_sem=back_recv.at[kind, offset],
            device_id=(dest, dp), device_id_type=MESH,
        )
        return remote, pltpu.make_async_copy(src, dst, back_recv.at[kind, offset])

    def attend(i, carry):
        block = (me + 1 + i) % n_seq
        where = pl.ds(pl.multiple_of(block * rows, rows), rows)
        outs = []
        for h in range(n_heads):
            scores = jnp.dot(queries[h, where, :], keys_t[h], preferred_element_type=jnp.float32)
            top = jnp.max(scores, axis=-1, keepdims=True)
            weight = jnp.exp2((scores - top) * scale).astype(jnp.bfloat16)
            summed = jnp.dot(weight, values[h], preferred_element_type=jnp.float32)
            outs.append((summed[:, :head_size] / summed[:, head_size : head_size + 1]).astype(jnp.bfloat16))
        attended[where, :] = jnp.concatenate(outs, axis=1)
        for kind, shift in enumerate((0, 1, n_seq - 1)):
            offset = (i + 1 + shift) % n_seq

            @pl.when(offset != 0)
            def _():
                back(kind, offset)[0].start()

            @pl.when(offset == 0)
            def _():
                back(kind, offset)[1].start()

        return carry

    lax.fori_loop(0, n_seq, attend, 0)

    for kind in range(3):
        back(kind, 0)[1].wait()
        for offset in range(1, n_seq):
            back(kind, offset)[0].wait()
    for copy in copies + forwards:
        copy.wait_send()


def attention(length, frames, gain, w, n_seq, n_dp, head_size):
    rows, width = frames.shape
    total = n_seq * rows
    n_heads = w.shape[1] // (3 * head_size)
    half = n_seq // 2
    dma = pltpu.SemaphoreType.DMA
    return pl.pallas_call(
        functools.partial(attention_kernel, n_seq, n_dp, head_size),
        out_shape=(
            jax.ShapeDtypeStruct((n_seq, rows + 2 * HALO, n_heads * head_size), jnp.bfloat16),
            jax.ShapeDtypeStruct((2, HALO, width), jnp.bfloat16),
        ),
        in_specs=[
            pl.BlockSpec(memory_space=pltpu.SMEM),
            pl.BlockSpec(memory_space=pl.ANY),
            pl.BlockSpec(memory_space=pltpu.VMEM),
            pl.BlockSpec(memory_space=pl.ANY),
        ],
        out_specs=(pl.BlockSpec(memory_space=pl.ANY),) * 2,
        scratch_shapes=[
            pltpu.VMEM((rows, width), jnp.bfloat16),
            pltpu.VMEM((n_seq, rows, width), jnp.bfloat16),
            pltpu.VMEM(w.shape, jnp.bfloat16),
            pltpu.VMEM((total, w.shape[1]), jnp.float32),
            pltpu.VMEM((n_heads, 128, total), jnp.bfloat16),
            pltpu.VMEM((n_heads, total, 128), jnp.bfloat16),
            pltpu.VMEM((n_heads, total, 128), jnp.bfloat16),
            pltpu.VMEM((total, n_heads * head_size), jnp.bfloat16),
            dma, dma((3,)), dma((3,)), dma((2,)), dma((2,)),
            dma((half,)), dma((half,)), dma((half,)), dma((half,)),
            dma((3, n_seq)), dma((3, n_seq)),
        ],
        compiler_params=pltpu.CompilerParams(collective_id=0, has_side_effects=True, vmem_limit_bytes=LIMIT),
    )(length, frames, gain, w)


def finish_kernel(n_seq, n_dp, length_ref, parts, frames, halo, wo, gain, conv_w, out, mid, padded):
    me = lax.axis_index("seq")
    dp = lax.axis_index("dp")
    count, width = frames.shape
    tall = count + 2 * HALO
    share = n_seq // n_dp
    depth = parts.shape[2]
    taps = conv_w.shape[0]
    reach = (taps - 1) // 2
    cut = 512

    for c in range(width // cut):
        columns = slice(c * cut, (c + 1) * cut)
        total = jnp.concatenate(
            [halo[0, :, columns], frames[:, columns], halo[1, :, columns]], axis=0
        ).astype(jnp.float32)
        for s in range(n_seq):
            slot = head_group(s, dp, n_seq, n_dp) * share + s % share
            rows = pl.ds(pl.multiple_of(slot * depth, depth), depth)
            total = total + jnp.dot(parts[s], wo[rows, columns], preferred_element_type=jnp.float32)
        mid[:, columns] = total

    part = 32

    def norm_part(i, carry):
        start = pl.multiple_of(i * part, part)
        where = pl.ds(start, part)
        values = mid[where, :]
        mean = jnp.mean(values, axis=-1, keepdims=True)
        centred = values - mean
        var = jnp.mean(centred * centred, axis=-1, keepdims=True)
        position = me * count - HALO + start + lax.broadcasted_iota(jnp.int32, (part, 1), 0)
        valid = (position >= 0) & (position < length_ref[0])
        normed = centred * lax.rsqrt(var + 1e-05) * gain[...]
        padded[where, :] = jnp.where(valid, normed, 0.0).astype(jnp.bfloat16).astype(jnp.float32)
        return carry

    lax.fori_loop(0, tall // part, norm_part, 0)

    lanes = 128

    def conv_part(c, carry):
        columns = pl.ds(pl.multiple_of(c * lanes, lanes), lanes)
        for half in range(count // 128):
            base = half * 128
            conv = jnp.zeros((128, lanes), jnp.float32)
            for turn in range(8):
                group = [tap for tap in range(taps) if (tap + HALO - reach) % 8 == turn]
                if not group:
                    continue
                low = (group[0] + HALO - reach) // 8 * 8
                high = (group[-1] + HALO - reach) // 8 * 8
                moved = padded[base + low + turn : base + high + turn + 128, columns]
                for tap in group:
                    first = (tap + HALO - reach) // 8 * 8 - low
                    conv = conv + conv_w[tap : tap + 1, columns] * moved[first : first + 128]
            result = mid[base + HALO : base + HALO + 128, columns] + conv * jax.nn.sigmoid(conv)
            out[base : base + 128, columns] = result.astype(jnp.bfloat16)
        return carry

    lax.fori_loop(0, width // lanes, conv_part, 0)


def finish(length, parts, frames, halo, wo, gain, conv_w, n_seq, n_dp):
    count, width = frames.shape
    return pl.pallas_call(
        functools.partial(finish_kernel, n_seq, n_dp),
        out_shape=jax.ShapeDtypeStruct((count, width), jnp.bfloat16),
        in_specs=[pl.BlockSpec(memory_space=pltpu.SMEM)] + [pl.BlockSpec(memory_space=pltpu.VMEM)] * 6,
        out_specs=pl.BlockSpec(memory_space=pltpu.VMEM),
        scratch_shapes=[
            pltpu.VMEM((count + 2 * HALO, width), jnp.float32),
            pltpu.VMEM((count + 2 * HALO, width), jnp.float32),
        ],
        compiler_params=pltpu.CompilerParams(vmem_limit_bytes=LIMIT),
    )(length, parts, frames, halo, wo, gain, conv_w)


def body(n_seq, n_dp, frames, lengths, wqkv, wo, gain_attn, gain_conv, conv_w):
    rows = frames[0]
    count, width = rows.shape
    head_size = width // HEADS
    share = n_seq // n_dp
    columns = wqkv.shape[1] // share
    seq = lax.axis_index("seq")
    w = lax.dynamic_slice_in_dim(wqkv, seq % share * columns, columns, axis=1)
    parts, halo = attention(lengths, rows, gain_attn[None], w, n_seq, n_dp, head_size)
    return finish(lengths, parts, rows, halo, wo, gain_conv[None], conv_w, n_seq, n_dp)[None]


def solution(mesh):
    return jax.shard_map(
        functools.partial(body, mesh.shape["seq"], mesh.shape["dp"]),
        mesh=mesh,
        in_specs=(P("dp", "seq", None), P("dp"), P(None, "dp"), P(), P(), P(), P()),
        out_specs=P("dp", "seq", None),
        check_vma=False,
    )
```

time: 116 us -> 92.7 us (0.80)
  Pallas kernels: 96.8 us -> 88.3 us
  matrix products: 8.12 us -> 0 us
  local copies, waits for them, and re-layouts: 9.84 us -> 2.93 us
    pallas_call x3 -> x1, Pallas kernels: 81.3 us -> 73 us  [attention(): pl.pallas_call(functools.partial(attention_kernel, n_seq, n_dp, head_size...]
    dot_general x1 -> x0, matrix products: 8.12 us -> none  [body(): jnp.dot(normed.reshape(n_seq * count, width), w, preferred_element_type=j...]
    convert_element_type x1 -> x0, local copies, waits for them, and re-layouts: 4.33 us -> none  [body(): qkv = jnp.dot(normed.reshape(n_seq * count, width), w, preferred_element_...]
    unnamed x18 -> x10, local copies, waits for them, and re-layouts: 4.59 us -> 2.01 us
where the time goes in v2:
time: 92.7 us; the launch traced here: 91.9 us
  Pallas kernels  88.3 us (95%)
  local copies, waits for them, and re-layouts  2.93 us (3%)
    pallas_call x1, Pallas kernels, attention(): pl.pallas_call(functools.partial(attention_kernel, n_seq, n_dp, head_size...  73 us
    pallas_call x1, Pallas kernels, finish(): pl.pallas_call(functools.partial(finish_kernel, n_seq, n_dp), out_shape=j...  15.3 us
    unnamed x10, local copies, waits for them, and re-layouts  2.01 us

profile of v2, /device:TPU:0, one launch (start us, length us, event | category | flops | bytes accessed | tf_op | source)
XLA Modules:
  0.0 91.9 jit_solution(8573400341724565833)
XLA Ops:
  0.0 0.0 copy-start
  0.0 0.0 copy-start.3
  0.0 0.0 copy-start.4
  0.0 2.0 %copy-done = bf16[1536,1152]{1,0:T(8,128)(2,1)S(1)} copy-done((bf16[1536,1152]{1,0:T(8,128)(2,1)S(1)}, bf16[1536,1152]{1,0:T(8,128)(2,1)}, u32[]{:S(2)}) %copy-start) | copy-done | bytes 3538968
  2.0 0.0 copy-start.1
  2.0 0.0 copy-start.2
  2.0 0.9 constant_dynamic-slice_fusion.w_ref
  3.6 0.0 copy-done.3
  3.6 0.0 copy-done.1
  3.6 73.0 %shard_map.73 = (bf16[8,288,192]{2,1,0:T(8,128)(2,1)S(1)}, bf16[2,16,1536]{2,1,0:T(8,128)(2,1)S(1)}) custom-call(s32[1]{0:T(128)S(6)} %copy.8.length_ref, bf16[256,1536]{1,0:T(8,128)(2,1)S(1)} %bitcast.2, f32[1,1536]{1,0:T(1,128)S(1)} %broadcast_in_dim.9.gain, bf16[1536,576]{1,0:T(8,128)(2,1)S(1)} %constant_dynamic-slice_fusion.w_ref), custom_call_target="tpu_custom_call" | custom-call | tf_op jit(solution)/shard_map/pallas_call | solution.py:230
  76.6 0.0 copy-done.4
  76.6 0.0 copy-done.2
  76.6 15.3 %shard_map.74 = bf16[256,1536]{1,0:T(8,128)(2,1)} custom-call(s32[1]{0:T(128)S(6)} %copy.8.length_ref, bf16[8,288,192]{2,1,0:T(8,128)(2,1)S(1)} %get-tuple-element.7.parts, bf16[256,1536]{1,0:T(8,128)(2,1)S(1)} %bitcast.3, bf16[2,16,1536]{2,1,0:T(8,128)(2,1)S(1)} %get-tuple-element.8.halo, bf16[1536,1536]{1,0:T(8,128)(2,1)} %wo.1, ...), custom_call_target="tpu_custom_call" | custom-call | tf_op jit(solution)/shard_map/pallas_call | solution.py:325
  (2 shorter events, 0.0 us)
Async XLA Ops:
  0.0 2.0 %copy-start = (bf16[1536,1152]{1,0:T(8,128)(2,1)S(1)}, bf16[1536,1152]{1,0:T(8,128)(2,1)}, u32[]{:S(2)}) copy-start(bf16[1536,1152]{1,0:T(8,128)(2,1)} %param.9) | copy-start | bytes 10616836
  0.0 3.6 %copy-start.3 = (f32[1536]{0:T(1024)S(1)}, f32[1536]{0:T(1024)}, u32[]{:S(2)}) copy-start(f32[1536]{0:T(1024)} %param.11) | copy-start | bytes 18436
  0.0 76.6 %copy-start.4 = (f32[1536]{0:T(1024)S(1)}, f32[1536]{0:T(1024)}, u32[]{:S(2)}) copy-start(f32[1536]{0:T(1024)} %param.12) | copy-start | bytes 18436
  2.0 1.6 %copy-start.1 = (bf16[1,256,1536]{2,1,0:T(8,128)(2,1)S(1)}, bf16[1,256,1536]{2,1,0:T(8,128)(2,1)}, u32[]{:S(2)}) copy-start(bf16[1,256,1536]{2,1,0:T(8,128)(2,1)} %param.7) | copy-start | bytes 2359300
  2.0 74.6 %copy-start.2 = (f32[31,1536]{1,0:T(8,128)S(1)}, f32[31,1536]{1,0:T(8,128)}, u32[]{:S(2)}) copy-start(f32[31,1536]{1,0:T(8,128)} %conv_w.1) | copy-start | bytes 571396

commit v3 on v2

v3 whole, which is shorter than its diff:
```python
import functools

import jax
import jax.numpy as jnp
from jax import lax
from jax.experimental import pallas as pl
from jax.experimental.pallas import tpu as pltpu
from jax.sharding import PartitionSpec as P

HEADS = 16
HALO = 16
MESH = pl.DeviceIdType.MESH


def reversed_bits(value, count):
    bits = count.bit_length() - 1
    out = 0
    for i in range(bits):
        out = out + (value // (1 << i)) % 2 * (1 << (bits - 1 - i))
    return out


def head_group(seq, dp, n_seq, n_dp):
    column = seq // (n_seq // n_dp)
    return (reversed_bits(dp, n_dp) + column) % n_dp


def attention_kernel(
    n_seq, n_dp, head_size, pieces, length_ref, frames_ref, gain, gain_conv, conv_w, w_ref, wo_ref, out,
    parts, halo_out, wo_out, mid, padded, heads,
    frames, normed, w_full, keys_t, values, queries, attended,
    frame_sem, w_sem, wo_sem, w_send, w_recv, halo_send, halo_recv,
    send_sem, recv_sem, forward_send, forward_recv, back_send, back_recv, *w_parts,
):
    count = len(pieces)
    w_own, w_got = w_parts[:count], w_parts[count:]
    me = lax.axis_index("seq")
    dp = lax.axis_index("dp")
    rows, width = frames.shape
    total = n_seq * rows
    half = n_seq // 2
    column = me // (n_seq // n_dp)
    source = head_group(me, dp, n_seq, n_dp)
    target = reversed_bits((dp + n_dp - column) % n_dp, n_dp)
    sibling = me + 1 - 2 * (me % 2)
    left = (me + n_seq - 1) % n_seq
    right = (me + 1) % n_seq
    peers = [(me + 2 * i) % n_seq for i in range(1, half)]
    n_heads = attended.shape[0]
    share = n_seq // n_dp
    wide = 128

    w_load = pltpu.make_async_copy(w_ref, w_full, w_sem)
    w_load.start()
    load = pltpu.make_async_copy(frames_ref, frames, frame_sem)
    load.start()
    barrier = pltpu.get_barrier_semaphore()
    for i in range(1, n_seq):
        pl.semaphore_signal(barrier, inc=1, device_id=((me + i) % n_seq, dp), device_id_type=MESH)

    @pl.when(target != dp)
    def _():
        pl.semaphore_signal(barrier, inc=1, device_id=(me, source), device_id_type=MESH)
        pl.semaphore_signal(barrier, inc=1, device_id=(me, target), device_id_type=MESH)
        pl.semaphore_wait(barrier, n_seq + 1)

    @pl.when(target == dp)
    def _():
        pl.semaphore_wait(barrier, n_seq - 1)

    def weights(c):
        return pltpu.make_async_remote_copy(
            src_ref=w_own[c], dst_ref=w_got[c], send_sem=w_send.at[c], recv_sem=w_recv.at[c],
            device_id=(me, target), device_id_type=MESH,
        )

    def kept(c):
        return pltpu.make_async_copy(w_own[c], w_got[c], w_recv.at[c])

    w_load.wait()
    for c in range(count):
        for j in range(share):
            @pl.when(me % share == j)
            def _():
                def cut(i, carry):
                    where = pl.ds(pl.multiple_of(i * 256, 256), 256)
                    w_own[c][where, :] = jnp.concatenate(
                        [
                            w_full[where, ((j * n_heads + h) * 3 + p) * head_size : ((j * n_heads + h) * 3 + p + 1) * head_size]
                            for h, p in pieces[c]
                        ],
                        axis=1,
                    )
                    return carry

                lax.fori_loop(0, width // 256, cut, 0)

        @pl.when(target != dp)
        def _():
            weights(c).start()

        @pl.when(target == dp)
        def _():
            kept(c).start()

    load.wait()
    part = 64

    def norm_part(i, carry):
        where = pl.ds(pl.multiple_of(i * part, part), part)
        numbers = frames[where, :].astype(jnp.float32)
        mean = jnp.mean(numbers, axis=-1, keepdims=True)
        centred = numbers - mean
        var = jnp.mean(centred * centred, axis=-1, keepdims=True)
        normed[me, where, :] = (centred * lax.rsqrt(var + 1e-05) * gain[...]).astype(jnp.bfloat16)
        return carry

    lax.fori_loop(0, rows // part, norm_part, 0)

    copies = []
    for i in range(half):
        copies.append(pltpu.make_async_remote_copy(
            src_ref=normed.at[me], dst_ref=normed.at[me], send_sem=send_sem.at[i], recv_sem=recv_sem.at[i],
            device_id=(peers[i - 1] if i else sibling, dp), device_id_type=MESH,
        ))
    copies.append(pltpu.make_async_remote_copy(
        src_ref=frames.at[pl.ds(0, HALO)], dst_ref=halo_out.at[1],
        send_sem=halo_send.at[0], recv_sem=halo_recv.at[0],
        device_id=(left, dp), device_id_type=MESH,
    ))
    copies.append(pltpu.make_async_remote_copy(
        src_ref=frames.at[pl.ds(rows - HALO, HALO)], dst_ref=halo_out.at[0],
        send_sem=halo_send.at[1], recv_sem=halo_recv.at[1],
        device_id=(right, dp), device_id_type=MESH,
    ))
    for copy in copies[1:] + copies[:1]:
        copy.start()

    depth = n_heads * head_size
    reorders = []
    for i in range(n_seq):
        slot = head_group(i, dp, n_seq, n_dp) * share + i % share
        reorder = pltpu.make_async_copy(
            wo_ref.at[pl.ds(pl.multiple_of(slot * depth, depth), depth)],
            wo_out.at[pl.ds(i * depth, depth)],
            wo_sem.at[i],
        )
        reorder.start()
        reorders.append(reorder)

    forwards = []
    for i in range(1, half):
        origin = (me + n_seq - 2 * i) % n_seq
        copies[i].wait_recv()
        forward = pltpu.make_async_remote_copy(
            src_ref=normed.at[origin], dst_ref=normed.at[origin],
            send_sem=forward_send.at[i], recv_sem=forward_recv.at[i],
            device_id=(sibling, dp), device_id_type=MESH,
        )
        forward.start()
        forwards.append(forward)
    for copy in copies[:1] + copies[half:]:
        copy.wait_recv()
    for forward in forwards:
        forward.wait_recv()

    scale = head_size ** (-0.5) * 1.4426950408889634
    places = [(0, rows, HALO), (rows - HALO, HALO, 0), (0, HALO, rows + HALO)]

    def back(kind, h, offset):
        dest = (me + offset) % n_seq
        block = (dest + n_seq - (0, 1, n_seq - 1)[kind]) % n_seq
        first, size, at = places[kind]
        src = attended.at[h, pl.ds(pl.multiple_of(block * rows + first, HALO), size)]
        dst = parts.at[me, h, pl.ds(at, size)]
        row = kind * n_heads + h
        remote = pltpu.make_async_remote_copy(
            src_ref=src, dst_ref=dst, send_sem=back_send.at[row, offset], recv_sem=back_recv.at[row, offset],
            device_id=(dest, dp), device_id_type=MESH,
        )
        return remote, pltpu.make_async_copy(src, dst, back_recv.at[row, offset])

    for c in range(count):
        @pl.when(target != dp)
        def _():
            weights(c).wait()

        @pl.when(target == dp)
        def _():
            kept(c).wait()

        def product(s, carry):
            where = pl.ds(pl.multiple_of(s * rows, rows), rows)
            qkv = jnp.dot(normed[s], w_got[c][...], preferred_element_type=jnp.float32).astype(jnp.bfloat16)
            extra = lax.broadcasted_iota(jnp.int32, (rows, wide - head_size), 1)
            row = s * rows + lax.broadcasted_iota(jnp.int32, (rows, wide - head_size), 0)
            first = extra == 0
            ones = jnp.where(first, 1.0, 0.0).astype(jnp.bfloat16)
            bias = jnp.where(first & (row >= length_ref[0]), -1e30, 0.0).astype(jnp.bfloat16)
            for i, (h, p) in enumerate(pieces[c]):
                one = qkv[:, i * head_size : (i + 1) * head_size]
                if p == 0:
                    queries[h, where, :] = jnp.concatenate([one, ones], axis=1)
                elif p == 1:
                    keys_t[h, :, where] = jnp.concatenate([one, bias], axis=1).T
                else:
                    values[h, where, :] = jnp.concatenate([one, ones], axis=1)
            return carry

        lax.fori_loop(0, n_seq, product, 0)
        ready = [h for h in range(n_heads) if (h, 0) in pieces[c]]

        def attend(i, carry):
            block = (me + 1 + i) % n_seq
            where = pl.ds(pl.multiple_of(block * rows, rows), rows)
            for h in ready:
                scores = jnp.dot(queries[h, where, :], keys_t[h], preferred_element_type=jnp.float32)
                top = jnp.max(scores, axis=-1, keepdims=True)
                weight = jnp.exp2((scores - top) * scale).astype(jnp.bfloat16)
                summed = jnp.dot(weight, values[h], preferred_element_type=jnp.float32)
                attended[h, where, :] = (
                    summed[:, :head_size] / summed[:, head_size : head_size + 1]
                ).astype(jnp.bfloat16)
                for kind, shift in enumerate((0, 1, n_seq - 1)):
                    offset = (i + 1 + shift) % n_seq

                    @pl.when(offset != 0)
                    def _():
                        back(kind, h, offset)[0].start()

                    @pl.when(offset == 0)
                    def _():
                        back(kind, h, offset)[1].start()

            return carry

        lax.fori_loop(0, n_seq, attend, 0)

    for h in range(n_heads):
        for kind in range(3):
            back(kind, h, 0)[1].wait()
            for offset in range(1, n_seq):
                back(kind, h, offset)[0].wait()
    for reorder in reorders:
        reorder.wait()
    for copy in copies + forwards:
        copy.wait_send()
    finish(n_seq, length_ref, parts, frames, halo_out, wo_out, gain_conv, conv_w, out, mid, padded, heads)


def attention(length, frames, gain, gain_conv, conv_w, w, wo, n_seq, n_dp, head_size):
    rows, width = frames.shape
    total = n_seq * rows
    n_heads = w.shape[1] // (n_seq // n_dp) // (3 * head_size)
    half = n_seq // 2
    dma = pltpu.SemaphoreType.DMA
    if n_heads == 2:
        pieces = (((0, 0), (0, 1), (0, 2), (1, 1)), ((1, 0), (1, 2)))
    else:
        pieces = (tuple((h, p) for h in range(n_heads) for p in range(3)),)
    count = len(pieces)
    return pl.pallas_call(
        functools.partial(attention_kernel, n_seq, n_dp, head_size, pieces),
        out_shape=jax.ShapeDtypeStruct((rows, width), jnp.bfloat16),
        in_specs=[
            pl.BlockSpec(memory_space=pltpu.SMEM),
            pl.BlockSpec(memory_space=pltpu.HBM),
            pl.BlockSpec(memory_space=pltpu.VMEM),
            pl.BlockSpec(memory_space=pltpu.VMEM),
            pl.BlockSpec(memory_space=pltpu.VMEM),
            pl.BlockSpec(memory_space=pltpu.HBM),
            pl.BlockSpec(memory_space=pltpu.HBM),
        ],
        out_specs=pl.BlockSpec(memory_space=pltpu.VMEM),
        scratch_shapes=[
            pltpu.VMEM((n_seq, n_heads, rows + 2 * HALO, head_size), jnp.bfloat16),
            pltpu.VMEM((2, HALO, width), jnp.bfloat16),
            pltpu.VMEM(wo.shape, jnp.bfloat16),
            pltpu.VMEM((rows + 2 * HALO, width), jnp.float32),
            pltpu.VMEM((rows + 2 * HALO, width), jnp.float32),
            pltpu.VMEM((rows + 2 * HALO, width), jnp.bfloat16),
            pltpu.VMEM((rows, width), jnp.bfloat16),
            pltpu.VMEM((n_seq, rows, width), jnp.bfloat16),
            pltpu.VMEM(w.shape, jnp.bfloat16),
            pltpu.VMEM((n_heads, 128, total), jnp.bfloat16),
            pltpu.VMEM((n_heads, total, 128), jnp.bfloat16),
            pltpu.VMEM((n_heads, total, 128), jnp.bfloat16),
            pltpu.VMEM((n_heads, total, head_size), jnp.bfloat16),
            dma, dma, dma((n_seq,)), dma((count,)), dma((count,)), dma((2,)), dma((2,)),
            dma((half,)), dma((half,)), dma((half,)), dma((half,)),
            dma((3 * n_heads, n_seq)), dma((3 * n_heads, n_seq)),
        ]
        + [pltpu.VMEM((width, len(piece) * head_size), jnp.bfloat16) for piece in pieces] * 2,
        compiler_params=pltpu.CompilerParams(
            collective_id=0, has_side_effects=True, vmem_limit_bytes=58 * 1024 * 1024
        ),
    )(length, frames, gain, gain_conv, conv_w, w, wo)


def finish(n_seq, length_ref, parts, frames, halo, wo, gain, conv_w, out, mid, padded, heads):
    me = lax.axis_index("seq")
    count, width = frames.shape
    tall = count + 2 * HALO
    taps = conv_w.shape[0]
    reach = (taps - 1) // 2
    cut = 512
    heads[...] = jnp.concatenate(
        [parts[s, h] for s in range(n_seq) for h in range(parts.shape[1])], axis=1
    )
    for c in range(width // cut):
        columns = slice(c * cut, (c + 1) * cut)
        rows = jnp.concatenate([halo[0, :, columns], frames[:, columns], halo[1, :, columns]], axis=0)
        mid[:, columns] = rows.astype(jnp.float32) + jnp.dot(
            heads[...], wo[:, columns], preferred_element_type=jnp.float32
        )

    part = 96

    def norm_part(i, carry):
        start = pl.multiple_of(i * part, part)
        where = pl.ds(start, part)
        values = mid[where, :]
        mean = jnp.mean(values, axis=-1, keepdims=True)
        centred = values - mean
        var = jnp.mean(centred * centred, axis=-1, keepdims=True)
        position = me * count - HALO + start + lax.broadcasted_iota(jnp.int32, (part, 1), 0)
        valid = (position >= 0) & (position < length_ref[0])
        normed = centred * lax.rsqrt(var + 1e-05) * gain[...]
        padded[where, :] = jnp.where(valid, normed, 0.0).astype(jnp.bfloat16).astype(jnp.float32)
        return carry

    lax.fori_loop(0, tall // part, norm_part, 0)

    lanes = 128

    def conv_part(c, carry):
        columns = pl.ds(pl.multiple_of(c * lanes, lanes), lanes)
        for half in range(count // 128):
            base = half * 128
            conv = jnp.zeros((128, lanes), jnp.float32)
            for turn in range(8):
                group = [tap for tap in range(taps) if (tap + HALO - reach) % 8 == turn]
                if not group:
                    continue
                low = (group[0] + HALO - reach) // 8 * 8
                high = (group[-1] + HALO - reach) // 8 * 8
                moved = padded[base + low + turn : base + high + turn + 128, columns]
                for tap in group:
                    first = (tap + HALO - reach) // 8 * 8 - low
                    conv = conv + conv_w[tap : tap + 1, columns] * moved[first : first + 128]
            result = mid[base + HALO : base + HALO + 128, columns] + conv * jax.nn.sigmoid(conv)
            out[base : base + 128, columns] = result.astype(jnp.bfloat16)
        return carry

    lax.fori_loop(0, width // lanes, conv_part, 0)


def body(n_seq, n_dp, frames, lengths, wqkv, wo, gain_attn, gain_conv, conv_w):
    rows = frames[0]
    count, width = rows.shape
    head_size = width // HEADS
    return attention(
        lengths, rows, gain_attn[None], gain_conv[None], conv_w, wqkv, wo, n_seq, n_dp, head_size
    )[None]


def solution(mesh):
    return jax.shard_map(
        functools.partial(body, mesh.shape["seq"], mesh.shape["dp"]),
        mesh=mesh,
        in_specs=(P("dp", "seq", None), P("dp"), P(None, "dp"), P(), P(), P(), P()),
        out_specs=P("dp", "seq", None),
        check_vma=False,
    )
```

time: 92.7 us -> 94.4 us (1.018)
  local copies, waits for them, and re-layouts: 2.93 us -> 4.65 us
    pallas_call x1, Pallas kernels: 73 us -> 88.8 us  [attention(): pl.pallas_call(functools.partial(attention_kernel, n_seq, n_dp, head_size...]
    pallas_call x1 -> x0, Pallas kernels: 15.3 us -> none  [finish(): pl.pallas_call(functools.partial(finish_kernel, n_seq, n_dp), out_shape=j...]
    broadcast_in_dim x1, local copies, waits for them, and re-layouts: 0.01 us -> 1.29 us  [body(): gain_attn[None]]
    broadcast_in_dim x1, local copies, waits for them, and re-layouts: 0.01 us -> 1.29 us  [body(): gain_conv[None]]
    unnamed x10 -> x1, local copies, waits for them, and re-layouts: 2.01 us -> 2.06 us
where the time goes in v3:
time: 94.4 us; the launch traced here: 94.1 us
  Pallas kernels  88.8 us (94%)
  local copies, waits for them, and re-layouts  4.65 us (5%)
    pallas_call x1, Pallas kernels, attention(): pl.pallas_call(functools.partial(attention_kernel, n_seq, n_dp, head_size...  88.8 us
    unnamed x1, local copies, waits for them, and re-layouts  2.06 us

profile of v3, /device:TPU:0, one launch (start us, length us, event | category | flops | bytes accessed | tf_op | source)
XLA Modules:
  0.0 94.1 jit_solution(8726612004331697562)
XLA Ops:
  0.7 1.3 %broadcast_in_dim.9.gain = f32[1,1536]{1,0:T(1,128)} reshape(f32[1536]{0:T(1024)} %param.11) | data formatting | bytes 12288 | tf_op jit(solution)/shard_map/broadcast_in_dim | solution.py:363
  1.9 1.3 %broadcast_in_dim.10.gain_conv = f32[1,1536]{1,0:T(1,128)} reshape(f32[1536]{0:T(1024)} %param.12) | data formatting | bytes 12288 | tf_op jit(solution)/shard_map/broadcast_in_dim | solution.py:363
  3.2 88.8 %shard_map.73 = bf16[256,1536]{1,0:T(8,128)(2,1)} custom-call(s32[1]{0:T(128)S(6)} %copy.9.length_ref, bf16[256,1536]{1,0:T(8,128)(2,1)} %bitcast.3, f32[1,1536]{1,0:T(1,128)} %broadcast_in_dim.9.gain, f32[1,1536]{1,0:T(1,128)} %broadcast_in_dim.10.gain_conv, f32[31,1536]{1,0:T(8,128)} %conv_w.1, bf16[1536,1152]{1,0:T(8,128)(2,1)} %w_ref.1, ...), custom_call_target="tpu_custom_call" | custom-call | tf_op jit(solution)/shard_map/pallas_call | solution.py:262
  92.0 2.1 %copy.10 = bf16[1,256,1536]{2,1,0:T(8,128)(2,1)} copy(bf16[1,256,1536]{2,1,0:T(8,128)(2,1)} %bitcast.2) | data formatting | bytes 1572864

commit v4 on v3

--- a/solution.py
+++ b/solution.py
@@ -95,9 +95,10 @@
 
                 lax.fori_loop(0, width // 256, cut, 0)
 
-        @pl.when(target != dp)
-        def _():
-            weights(c).start()
+        if c == 0:
+            @pl.when(target != dp)
+            def _():
+                weights(c).start()
 
         @pl.when(target == dp)
         def _():
@@ -112,7 +113,7 @@
         mean = jnp.mean(numbers, axis=-1, keepdims=True)
         centred = numbers - mean
         var = jnp.mean(centred * centred, axis=-1, keepdims=True)
-        normed[me, where, :] = (centred * lax.rsqrt(var + 1e-05) * gain[...]).astype(jnp.bfloat16)
+        normed[me, where, :] = (centred * lax.rsqrt(var + 1e-05) * gain[...][None, :]).astype(jnp.bfloat16)
         return carry
 
     lax.fori_loop(0, rows // part, norm_part, 0)
@@ -159,6 +160,12 @@
         )
         forward.start()
         forwards.append(forward)
+        if i == 1:
+            @pl.when(target != dp)
+            def _():
+                for c in range(1, count):
+                    weights(c - 1).wait_send()
+                    weights(c).start()
     for copy in copies[:1] + copies[half:]:
         copy.wait_recv()
     for forward in forwards:
@@ -183,7 +190,9 @@
     for c in range(count):
         @pl.when(target != dp)
         def _():
-            weights(c).wait()
+            weights(c).wait_recv()
+            if c == count - 1:
+                weights(c).wait_send()
 
         @pl.when(target == dp)
         def _():
@@ -210,31 +219,34 @@
         lax.fori_loop(0, n_seq, product, 0)
         ready = [h for h in range(n_heads) if (h, 0) in pieces[c]]
 
-        def attend(i, carry):
-            block = (me + 1 + i) % n_seq
-            where = pl.ds(pl.multiple_of(block * rows, rows), rows)
+        def attend(pair, carry):
             for h in ready:
-                scores = jnp.dot(queries[h, where, :], keys_t[h], preferred_element_type=jnp.float32)
-                top = jnp.max(scores, axis=-1, keepdims=True)
-                weight = jnp.exp2((scores - top) * scale).astype(jnp.bfloat16)
-                summed = jnp.dot(weight, values[h], preferred_element_type=jnp.float32)
-                attended[h, where, :] = (
-                    summed[:, :head_size] / summed[:, head_size : head_size + 1]
-                ).astype(jnp.bfloat16)
-                for kind, shift in enumerate((0, 1, n_seq - 1)):
-                    offset = (i + 1 + shift) % n_seq
-
-                    @pl.when(offset != 0)
-                    def _():
-                        back(kind, h, offset)[0].start()
-
-                    @pl.when(offset == 0)
-                    def _():
-                        back(kind, h, offset)[1].start()
+                for i in (2 * pair, 2 * pair + 1):
+                    block = (me + 1 + i) % n_seq
+                    where = pl.ds(pl.multiple_of(block * rows, rows), rows)
+                    scores = jnp.dot(queries[h, where, :], keys_t[h], preferred_element_type=jnp.float32)
+                    top = jnp.max(scores, axis=-1, keepdims=True)
+                    weight = jnp.exp2((scores - top) * scale).astype(jnp.bfloat16)
+                    summed = jnp.dot(weight, values[h], preferred_element_type=jnp.float32)
+                    attended[h, where, :] = (
+                        summed[:, :head_size] / summed[:, head_size : head_size + 1]
+                    ).astype(jnp.bfloat16)
+            for h in ready:
+                for i in (2 * pair, 2 * pair + 1):
+                    for kind, shift in enumerate((0, 1, n_seq - 1)):
+                        offset = (i + 1 + shift) % n_seq
+
+                        @pl.when(offset != 0)
+                        def _():
+                            back(kind, h, offset)[0].start()
+
+                        @pl.when(offset == 0)
+                        def _():
+                            back(kind, h, offset)[1].start()
 
             return carry
 
-        lax.fori_loop(0, n_seq, attend, 0)
+        lax.fori_loop(0, n_seq // 2, attend, 0)
 
     for h in range(n_heads):
         for kind in range(3):
@@ -325,7 +337,7 @@
         var = jnp.mean(centred * centred, axis=-1, keepdims=True)
         position = me * count - HALO + start + lax.broadcasted_iota(jnp.int32, (part, 1), 0)
         valid = (position >= 0) & (position < length_ref[0])
-        normed = centred * lax.rsqrt(var + 1e-05) * gain[...]
+        normed = centred * lax.rsqrt(var + 1e-05) * gain[...][None, :]
         padded[where, :] = jnp.where(valid, normed, 0.0).astype(jnp.bfloat16).astype(jnp.float32)
         return carry
 
@@ -360,7 +372,7 @@
     count, width = rows.shape
     head_size = width // HEADS
     return attention(
-        lengths, rows, gain_attn[None], gain_conv[None], conv_w, wqkv, wo, n_seq, n_dp, head_size
+        lengths, rows, gain_attn, gain_conv, conv_w, wqkv, wo, n_seq, n_dp, head_size
     )[None]
 
 

time: 94.4 us -> 91.2 us (0.966)
  local copies, waits for them, and re-layouts: 4.65 us -> 2.06 us
    broadcast_in_dim x2 -> x0, local copies, waits for them, and re-layouts: 2.58 us -> none  [the longest x1 1.29 us: body(): gain_attn[None]]
where the time goes in v4:
time: 91.2 us; the launch traced here: 91.1 us
  Pallas kernels  88.3 us (97%)
  local copies, waits for them, and re-layouts  2.06 us (2%)
    pallas_call x1, Pallas kernels, attention(): pl.pallas_call(functools.partial(attention_kernel, n_seq, n_dp, head_size...  88.3 us
    unnamed x1, local copies, waits for them, and re-layouts  2.06 us

profile of v4, /device:TPU:0, one launch (start us, length us, event | category | flops | bytes accessed | tf_op | source)
XLA Modules:
  0.0 91.1 jit_solution(5685011445375777558)
XLA Ops:
  0.7 88.3 %shard_map.73 = bf16[256,1536]{1,0:T(8,128)(2,1)} custom-call(s32[1]{0:T(128)S(6)} %copy.9.length_ref, bf16[256,1536]{1,0:T(8,128)(2,1)} %bitcast.3, f32[1536]{0:T(1024)} %gain.1, f32[1536]{0:T(1024)} %gain_conv.1, f32[31,1536]{1,0:T(8,128)} %conv_w.1, bf16[1536,1152]{1,0:T(8,128)(2,1)} %w_ref.1, bf16[1536,1536]{1,0:T(8,128)(2,1)} %wo_ref.1), custom_call_target="tpu_custom_call" | custom-call | tf_op jit(solution)/shard_map/pallas_call | solution.py:274
  89.0 2.1 %copy.10 = bf16[1,256,1536]{2,1,0:T(8,128)(2,1)} copy(bf16[1,256,1536]{2,1,0:T(8,128)(2,1)} %bitcast.2) | data formatting | bytes 1572864

commit v5 on v4

--- a/solution.py
+++ b/solution.py
@@ -77,33 +77,6 @@
     def kept(c):
         return pltpu.make_async_copy(w_own[c], w_got[c], w_recv.at[c])
 
-    w_load.wait()
-    for c in range(count):
-        for j in range(share):
-            @pl.when(me % share == j)
-            def _():
-                def cut(i, carry):
-                    where = pl.ds(pl.multiple_of(i * 256, 256), 256)
-                    w_own[c][where, :] = jnp.concatenate(
-                        [
-                            w_full[where, ((j * n_heads + h) * 3 + p) * head_size : ((j * n_heads + h) * 3 + p + 1) * head_size]
-                            for h, p in pieces[c]
-                        ],
-                        axis=1,
-                    )
-                    return carry
-
-                lax.fori_loop(0, width // 256, cut, 0)
-
-        if c == 0:
-            @pl.when(target != dp)
-            def _():
-                weights(c).start()
-
-        @pl.when(target == dp)
-        def _():
-            kept(c).start()
-
     load.wait()
     part = 64
 
@@ -136,6 +109,33 @@
     ))
     for copy in copies[1:] + copies[:1]:
         copy.start()
+
+    w_load.wait()
+    for c in range(count):
+        for j in range(share):
+            @pl.when(me % share == j)
+            def _():
+                def cut(i, carry):
+                    where = pl.ds(pl.multiple_of(i * 256, 256), 256)
+                    w_own[c][where, :] = jnp.concatenate(
+                        [
+                            w_full[where, ((j * n_heads + h) * 3 + p) * head_size : ((j * n_heads + h) * 3 + p + 1) * head_size]
+                            for h, p in pieces[c]
+                        ],
+                        axis=1,
+                    )
+                    return carry
+
+                lax.fori_loop(0, width // 256, cut, 0)
+
+        if c == 0:
+            @pl.when(target != dp)
+            def _():
+                weights(c).start()
+
+        @pl.when(target == dp)
+        def _():
+            kept(c).start()
 
     depth = n_heads * head_size
     reorders = []

time: 91.2 us -> 88.2 us (0.967)
  Pallas kernels: 88.3 us -> 85.3 us
    pallas_call x1, Pallas kernels: 88.3 us -> 85.3 us  [attention(): pl.pallas_call(functools.partial(attention_kernel, n_seq, n_dp, head_size...]
where the time goes in v5:
time: 88.2 us; the launch traced here: 88 us
  Pallas kernels  85.3 us (97%)
  local copies, waits for them, and re-layouts  2.06 us (2%)
    pallas_call x1, Pallas kernels, attention(): pl.pallas_call(functools.partial(attention_kernel, n_seq, n_dp, head_size...  85.3 us
    unnamed x1, local copies, waits for them, and re-layouts  2.06 us

profile of v5, /device:TPU:0, one launch (start us, length us, event | category | flops | bytes accessed | tf_op | source)
XLA Modules:
  0.0 88.0 jit_solution(15468317439790338488)
XLA Ops:
  0.7 85.3 %shard_map.73 = bf16[256,1536]{1,0:T(8,128)(2,1)} custom-call(s32[1]{0:T(128)S(6)} %copy.9.length_ref, bf16[256,1536]{1,0:T(8,128)(2,1)} %bitcast.3, f32[1536]{0:T(1024)} %gain.1, f32[1536]{0:T(1024)} %gain_conv.1, f32[31,1536]{1,0:T(8,128)} %conv_w.1, bf16[1536,1152]{1,0:T(8,128)(2,1)} %w_ref.1, bf16[1536,1536]{1,0:T(8,128)(2,1)} %wo_ref.1), custom_call_target="tpu_custom_call" | custom-call | tf_op jit(solution)/shard_map/pallas_call | solution.py:274
  85.9 2.1 %copy.10 = bf16[1,256,1536]{2,1,0:T(8,128)(2,1)} copy(bf16[1,256,1536]{2,1,0:T(8,128)(2,1)} %bitcast.2) | data formatting | bytes 1572864
